TPU v7x, 512 devices: a whole 4x8x8 slice. The times are simulated.
512 devices in a mesh: dp: 32 (over x, y_lo, core), vocab: 16 (over z, y_hi).
Axes of the slice: x: 4, y: 8 (y_hi: 2, y_lo: 4; y = y_hi * 4 + y_lo), z: 8, core: 2. Of those that a mesh axis runs over, the one named last changes fastest.
Arguments:
- hidden: bfloat16 [7168, 4096], P('dp'), may hold values from -6 to 6
- head_weight: bfloat16 [4096, 16384], P('dp', 'vocab'), may hold values from -0.09375 to 0.09375
- head_bias: float32 [16384], P('vocab'), may hold values from -1 to 1
- lengths: int32 [64, 2], P('dp'), may hold values from 1 to 80, as said below
- positives: int32 [64], P('dp'), may hold values from 0 to 63, each once
Outputs:
- hidden_grad: bfloat16 [7168, 4096], P(('dp', 'vocab'))
Inputs may be any that keep to these rules, and one draw needn't show every extreme that they name: `lengths`: query counts are at most 32, passage counts at most 80; the first slots of each are used.
All inputs are finite; a program needn't handle non-finite values.
Results may differ from a plain program's by a relative error of at most 0.0064.
Values may be sent and summed in bfloat16 or wider, within the bound.
A program may use at most 64 MiB of HBM per device.

v0:
```python
import jax
import jax.numpy as jnp
from jax import lax
from jax.sharding import PartitionSpec as P

QLEN = 32
POOL_TEMP = 0.25
SCORE_TEMP = 0.01
LOSS_SCALE = 65536.0


def row_mask(lengths, rows_pair):
    position = lax.broadcasted_iota(jnp.int32, (1, rows_pair), 1)
    is_query = position < QLEN
    offset = jnp.where(is_query, position, position - QLEN)
    limit_len = jnp.where(is_query, lengths[:, 0:1], lengths[:, 1:2])
    return (offset < limit_len).astype(jnp.float32)


def pool_terms(logits, token_mask):
    softened = jax.nn.softplus(logits)
    boosted = token_mask[:, :, None] * jnp.exp(jnp.log1p(softened) / POOL_TEMP)
    return (softened, boosted)


def pooled_vectors(boosted, lengths):
    query_sum = jnp.sum(boosted[:, :QLEN], axis=1)
    passage_sum = jnp.sum(boosted[:, QLEN:], axis=1)
    query_vec = POOL_TEMP * jnp.log(query_sum / lengths[:, 0:1].astype(jnp.float32))
    passage_vec = POOL_TEMP * jnp.log(passage_sum / lengths[:, 1:2].astype(jnp.float32))
    return (query_vec, passage_vec, query_sum, passage_sum)


def score_grads(scores, positives, pair_count):
    row_max = jnp.max(scores, axis=1, keepdims=True)
    shifted = jnp.exp(scores - row_max)
    softmax_out = shifted / jnp.sum(shifted, axis=1, keepdims=True)
    target = (positives[:, None] == lax.broadcasted_iota(jnp.int32, (1, pair_count), 1)).astype(
        jnp.float32
    )
    return LOSS_SCALE * (softmax_out - target)


def logit_grads(logits, softened, boosted, query_sum, passage_sum, query_grad, passage_grad):
    pairs_here = logits.shape[0]
    rest_rows = logits.shape[1] - QLEN
    entries = logits.shape[2]
    query_side = jnp.broadcast_to((query_grad / query_sum)[:, None, :], (pairs_here, QLEN, entries))
    passage_side = jnp.broadcast_to(
        (passage_grad / passage_sum)[:, None, :], (pairs_here, rest_rows, entries)
    )
    per_token = jnp.concatenate([query_side, passage_side], axis=1)
    slope = jax.nn.sigmoid(logits) / (1.0 + softened)
    return (boosted * slope * per_token).astype(jnp.bfloat16)


def per_device(hidden, head_weight, head_bias, lengths, positives):
    pairs_dev = lengths.shape[0]
    rows_pair = hidden.shape[0] // pairs_dev
    slice_width = head_bias.shape[0]
    vocab_devices = lax.axis_size("vocab")
    pairs_all = pairs_dev * lax.axis_size("dp")
    score_scale = 1.0 / (SCORE_TEMP * (slice_width * vocab_devices))
    weights = lax.all_gather(head_weight, "dp", axis=0, tiled=True)
    flat_logits = jnp.dot(hidden, weights, preferred_element_type=jnp.float32) + head_bias
    logits = flat_logits.reshape(pairs_dev, rows_pair, slice_width)
    token_mask = row_mask(lengths, rows_pair)
    softened, boosted = pool_terms(logits, token_mask)
    query_vec, passage_vec, query_sum, passage_sum = pooled_vectors(boosted, lengths)
    query_vec = query_vec.astype(jnp.bfloat16)
    passage_vec = passage_vec.astype(jnp.bfloat16)
    passages = lax.all_gather(passage_vec, "dp", axis=0, tiled=True)
    partial_value = lax.dot_general(
        query_vec, passages, (((1,), (1,)), ((), ())), preferred_element_type=jnp.float32
    )
    scores = score_scale * lax.psum(partial_value, "vocab")
    score_grad = score_grads(scores, positives, pairs_all)
    query_grad = score_scale * jnp.dot(
        score_grad, passages.astype(jnp.float32), precision=lax.Precision.HIGHEST
    )
    query_wide = query_vec.astype(jnp.float32)
    picked = score_grad
    passage_grad = score_scale * lax.psum_scatter(
        lax.dot_general(
            picked, query_wide, (((0,), (0,)), ((), ())), precision=lax.Precision.HIGHEST
        ),
        "dp",
        scatter_dimension=0,
        tiled=True,
    )
    logit_grad = logit_grads(
        logits, softened, boosted, query_sum, passage_sum, query_grad, passage_grad
    )
    logit_grad = logit_grad.reshape(pairs_dev * rows_pair, slice_width)
    picked = logit_grad
    summed = lax.psum_scatter(
        lax.dot_general(
            picked, weights, (((1,), (1,)), ((), ())), preferred_element_type=jnp.float32
        ),
        "vocab",
        scatter_dimension=0,
        tiled=True,
    )
    return summed.astype(jnp.bfloat16)


def solution(mesh):
    return jax.shard_map(
        per_device,
        mesh=mesh,
        in_specs=(P("dp", None), P("dp", "vocab"), P("vocab"), P("dp", None), P("dp")),
        out_specs=P(("dp", "vocab"), None),
        check_vma=False,
    )
```

profile of v0, /device:TPU:94, one launch (start us, length us, event | category | flops | bytes accessed | tf_op | source)
XLA Modules:
  0.0 667.0 jit_solution(6639236065506254835)
XLA Ops:
  6.5 0.7 all-gather.3.cloned.1.call-update
  7.5 1.0 slice_reduce_fusion.3
  8.8 1.0 convert_reduce_fusion.1
  9.9 72.9 %all-gather.3.cloned.1.call-done = bf16[4096,1024]{1,0:T(8,128)(2,1)} async-done(((bf16[128,1024]{1,0:T(8,128)(2,1)}), bf16[4096,1024]{1,0:T(8,128)(2,1)}) %all-gather.3.cloned.1.call-update) | async-done | bytes 8388624 | tf_op jit(solution)/shard_map/all_gather | solution.py:64
  82.7 5.4 convolution_add_fusion
  88.2 0.9 fusion.5
  89.2 37.5 %all-gather = bf16[32,2,1024]{2,1,0:T(2,128)(2,1)S(1)} all-gather(bf16[1,2,1024]{2,1,0:T(2,128)(2,1)S(1)} %fusion.8), channel_id=1, replica_groups=mesh['dp'=32,'vocab'=16] {'dp'}, dimensions={0}, use_global_device_ids=true | all-gather | bytes 135168 | tf_op jit(solution)/shard_map/all_gather | solution.py:72
  126.8 0.2 fusion.14
  127.0 51.4 %psum.7 = f32[2,64]{1,0:T(2,128)S(1)} all-reduce(f32[2,64]{1,0:T(2,128)S(1)} %fusion.14), channel_id=1, replica_groups=mesh['dp'=32,'vocab'=16] {'vocab'}, use_global_device_ids=true, to_apply=%region_2.3 | all-reduce | flops 128 | bytes 1024 | tf_op jit(solution)/shard_map/psum | solution.py:76
  178.5 0.2 fusion.10
  178.7 1.1 fusion.11
  179.8 1.3 dynamic-slice
  181.8 0.2 fusion.1
  182.0 272.1 %all-reduce.5.cloned.1.call-done = f32[64,1024]{1,0:T(8,128)} async-done(((f32[64,1024]{1,0:T(8,128)}), f32[64,1024]{1,0:T(8,128)}) %all-reduce.5.cloned.1.call-update) | async-done | bytes 262160
  454.2 0.8 fusion.7
  455.1 1.1 fusion.6
  456.2 7.9 %fusion.15 = f32[224,4096]{1,0:T(8,128)} fusion(bf16[224,1024]{1,0:T(8,128)(2,1)S(1)} %fusion.6, bf16[4096,1024]{1,0:T(8,128)(2,1)} %all-gather.3.cloned.1.call-done), kind=kOutput, calls=%fused_computation.38 | convolution fusion | flops 1879048192 | bytes 12517376 | tf_op jit(solution)/shard_map/dot_general | solution.py:97
  464.1 181.7 %fusion = f32[16,4096]{1,0:T(8,128)S(1)} fusion(f32[224,4096]{1,0:T(8,128)} %fusion.15), kind=kCustom, calls=%all-reduce-scatter | all-reduce-scatter fusion | flops 1048577 | bytes 3934208
  645.8 3.3 collective-permute-start
  649.2 3.5 collective-permute-start.1
  652.7 1.3 dynamic-slice.6
  654.6 4.2 collective-permute-done.1
  658.8 0.6 concatenate.7
  659.4 0.7 dynamic-slice_convert_fusion
  (30 shorter events, 1.2 us)
Async XLA Ops:
  6.5 76.2 %copy-start = (bf16[224,4096]{1,0:T(8,128)(2,1)S(1)}, bf16[224,4096]{1,0:T(8,128)(2,1)}, u32[]{:S(2)}) copy-start(bf16[224,4096]{1,0:T(8,128)(2,1)} %param.5) | copy-start | bytes 5505028
  6.5 76.2 %all-gather.3.cloned.1.call-start = ((), (), s32[]{:S(2)}) async-start(), calls=%async_computation | async-start | bytes 8650752 | tf_op jit(solution)/shard_map/all_gather | solution.py:64
  7.3 446.9 %all-reduce.5.cloned.1.call-start = ((), (), s32[]{:S(2)}) async-start(), calls=%async_computation.1 | async-start | bytes 524288
  9.9 168.8 %copy-start.1 = (s32[2]{0:T(128)S(1)}, s32[2]{0:T(128)}, u32[]{:S(2)}) copy-start(s32[2]{0:T(128)} %param.9) | copy-start | bytes 28
  645.8 13.0 %collective-permute-start = (bf16[16,4096]{1,0:T(8,128)(2,1)S(1)}, bf16[16,4096]{1,0:T(8,128)(2,1)S(1)}, u32[]{:S(2)}, u32[]{:S(2)}) collective-permute-start(bf16[16,4096]{1,0:T(8,128)(2,1)S(1)} %convert), channel_id=1, source_target_pairs={{0,1},{1,2},{2,3},{3,4},{4,5},{5,6},{6,7},{7,8},{8,9},{9,10},{10,1... | collective-permute-start | bytes 393224
  649.2 9.7 %collective-permute-start.1 = (bf16[14,4096]{1,0:T(8,128)(2,1)S(1)}, bf16[14,4096]{1,0:T(8,128)(2,1)S(1)}, u32[]{:S(2)}, u32[]{:S(2)}) collective-permute-start(bf16[14,4096]{1,0:T(8,128)(2,1)S(1)} %slice.20), channel_id=1, source_target_pairs={{0,2},{1,3},{2,4},{3,5},{4,6},{5,7},{6,8},{7,9},{8,10},{9,11},{10,... | collective-permute-start | bytes 344072
Sparse Core Ops, SparseCore 0:
  9.5 73.1 all-gather.2
  179.9 274.1 all-reduce.4
where the time goes:
time: 667 us
  waiting for transfers between devices  350 us (52%)
  blocking collectives  271 us (41%)
  matrix products  14.9 us (2%)
  between operations  14.9 us (2%)
  starting transfers between devices  6.84 us (1%)
    unnamed x5, waiting for transfers between devices  277 us
    unnamed x1, blocking collectives  182 us
    all_gather x1, waiting for transfers between devices, per_device(): weights = lax.all_gather(head_weight, 'dp', axis=0, tiled=True)  72.9 us
    psum x1, blocking collectives, per_device(): scores = score_scale * lax.psum(partial_value, 'vocab')  51.4 us
    all_gather x1, blocking collectives, per_device(): passages = lax.all_gather(passage_vec, 'dp', axis=0, tiled=True)  37.5 us
  transfers between devices with their start and end apart: 4, of which 3 were waited for; matrix products, arithmetic and copies ran while one was open for 1% of the time, Pallas kernels for 0%

commit v1 on v0

--- a/solution.py
+++ b/solution.py
@@ -69,7 +69,9 @@
     query_vec, passage_vec, query_sum, passage_sum = pooled_vectors(boosted, lengths)
     query_vec = query_vec.astype(jnp.bfloat16)
     passage_vec = passage_vec.astype(jnp.bfloat16)
-    passages = lax.all_gather(passage_vec, "dp", axis=0, tiled=True)
+    passages = jnp.concatenate(
+        lax.all_to_all(jnp.stack([passage_vec] * lax.axis_size("dp")), "dp", 0, 0), axis=0
+    )
     partial_value = lax.dot_general(
         query_vec, passages, (((1,), (1,)), ((), ())), preferred_element_type=jnp.float32
     )

time: 667 us -> 643 us (0.964)
  blocking collectives: 271 us -> 233 us
  starting transfers between devices: 6.84 us -> 14.7 us
    all_gather x1 -> x0, blocking collectives: 37.5 us -> none  [per_device(): passages = lax.all_gather(passage_vec, 'dp', axis=0, tiled=True)]
    all_to_all x0 -> x1, starting transfers between devices: none -> 7.82 us  [per_device(): lax.all_to_all(jnp.stack([passage_vec] * lax.axis_size('dp')), 'dp', 0, 0)]
  transfers between devices with their start and end apart: 4 -> 5, of which waited for: 3 -> 4; matrix products, arithmetic and copies ran while one was open for 1% -> 1% of each run, Pallas kernels for 0% -> 0%
where the time goes in v1:
time: 643 us; the launch traced here: 642 us
  waiting for transfers between devices  352 us (55%)
  blocking collectives  233 us (36%)
  matrix products  14.9 us (2%)
  between operations  14.9 us (2%)
  starting transfers between devices  14.7 us (2%)
  local copies, waits for them, and re-layouts  7.18 us (1%)
    unnamed x5, waiting for transfers between devices  275 us
    unnamed x1, blocking collectives  182 us
    all_gather x1, waiting for transfers between devices, per_device(): weights = lax.all_gather(head_weight, 'dp', axis=0, tiled=True)  73.4 us
    psum x1, blocking collectives, per_device(): scores = score_scale * lax.psum(partial_value, 'vocab')  51.5 us
  transfers between devices with their start and end apart: 5, of which 4 were waited for; matrix products, arithmetic and copies ran while one was open for 1% of the time, Pallas kernels for 0%

profile of v1, /device:TPU:94, one launch (start us, length us, event | category | flops | bytes accessed | tf_op | source)
XLA Modules:
  0.0 642.1 jit_solution(9431244980472925280)
XLA Ops:
  6.5 0.7 all-gather.2.cloned.1.call-update
  7.3 1.0 convert_reduce_fusion.1
  8.2 1.0 slice_reduce_fusion.3
  9.3 73.4 %all-gather.2.cloned.1.call-done = bf16[4096,1024]{1,0:T(8,128)(2,1)} async-done(((bf16[128,1024]{1,0:T(8,128)(2,1)}), bf16[4096,1024]{1,0:T(8,128)(2,1)}) %all-gather.2.cloned.1.call-update) | async-done | bytes 8388624 | tf_op jit(solution)/shard_map/all_gather | solution.py:64
  82.7 5.4 convolution_add_fusion
  88.2 0.9 fusion.5
  89.1 1.0 copy-done.1
  90.2 0.7 stack.2
  90.9 7.8 %all-to-all-start = ((bf16[32,2,1024]{2,1,0:T(2,128)(2,1)}), bf16[32,2,1024]{2,1,0:T(2,128)(2,1)S(1)}, u32[]{:S(2)}, u32[]{:S(2)}) async-start(bf16[32,2,1024]{2,1,0:T(2,128)(2,1)} %stack.2), calls=%async_computation | async-start | bytes 262144 | tf_op jit(solution)/shard_map/all_to_all | solution.py:73
  99.3 1.0 slice_reduce_fusion.1
  100.3 3.1 all-to-all-done
  103.6 51.5 %psum.7 = f32[2,64]{1,0:T(2,128)S(1)} all-reduce(f32[2,64]{1,0:T(2,128)S(1)} %fusion.13), channel_id=1, replica_groups=mesh['dp'=32,'vocab'=16] {'vocab'}, use_global_device_ids=true, to_apply=%region_2.3 | all-reduce | flops 128 | bytes 1024 | tf_op jit(solution)/shard_map/psum | solution.py:78
  155.5 1.1 fusion.10
  156.6 1.3 dynamic-slice
  158.8 270.5 %all-reduce.5.cloned.1.call-done = f32[64,1024]{1,0:T(8,128)} async-done(((f32[64,1024]{1,0:T(8,128)}), f32[64,1024]{1,0:T(8,128)}) %all-reduce.5.cloned.1.call-update) | async-done | bytes 262160
  429.2 0.8 fusion.7
  430.2 1.1 fusion.6
  431.3 7.9 %fusion.14 = f32[224,4096]{1,0:T(8,128)} fusion(bf16[224,1024]{1,0:T(8,128)(2,1)S(1)} %fusion.6, bf16[4096,1024]{1,0:T(8,128)(2,1)} %all-gather.2.cloned.1.call-done), kind=kOutput, calls=%fused_computation.37 | convolution fusion | flops 1879048192 | bytes 12517376 | tf_op jit(solution)/shard_map/dot_general | solution.py:99
  439.2 181.7 %fusion = f32[16,4096]{1,0:T(8,128)S(1)} fusion(f32[224,4096]{1,0:T(8,128)} %fusion.14), kind=kCustom, calls=%all-reduce-scatter | all-reduce-scatter fusion | flops 1048577 | bytes 3934208
  620.9 3.3 collective-permute-start
  624.3 3.5 collective-permute-start.1
  627.8 1.3 dynamic-slice.6
  629.7 4.2 collective-permute-done.1
  634.5 0.7 dynamic-slice_convert_fusion
  (34 shorter events, 2.4 us)
Async XLA Ops:
  6.5 76.2 %copy-start = (bf16[224,4096]{1,0:T(8,128)(2,1)S(1)}, bf16[224,4096]{1,0:T(8,128)(2,1)}, u32[]{:S(2)}) copy-start(bf16[224,4096]{1,0:T(8,128)(2,1)} %param.5) | copy-start | bytes 5505028
  6.5 76.2 %all-gather.2.cloned.1.call-start = ((), (), s32[]{:S(2)}) async-start(), calls=%async_computation.1 | async-start | bytes 8650752 | tf_op jit(solution)/shard_map/all_gather | solution.py:64
  9.3 146.2 %copy-start.2 = (s32[2]{0:T(128)S(1)}, s32[2]{0:T(128)}, u32[]{:S(2)}) copy-start(s32[2]{0:T(128)} %param.9) | copy-start | bytes 28
  89.1 1.0 copy-start.1
  90.9 12.4 %all-to-all-start = ((bf16[32,2,1024]{2,1,0:T(2,128)(2,1)}), bf16[32,2,1024]{2,1,0:T(2,128)(2,1)S(1)}, u32[]{:S(2)}, u32[]{:S(2)}) async-start(bf16[32,2,1024]{2,1,0:T(2,128)(2,1)} %stack.2), calls=%async_computation | async-start | bytes 262144 | tf_op jit(solution)/shard_map/all_to_all | solution.py:73
  98.7 330.5 %all-reduce.5.cloned.1.call-start = ((), (), s32[]{:S(2)}) async-start(), calls=%async_computation.2 | async-start | bytes 524288
  620.9 13.0 %collective-permute-start = (bf16[16,4096]{1,0:T(8,128)(2,1)S(1)}, bf16[16,4096]{1,0:T(8,128)(2,1)S(1)}, u32[]{:S(2)}, u32[]{:S(2)}) collective-permute-start(bf16[16,4096]{1,0:T(8,128)(2,1)S(1)} %convert), channel_id=1, source_target_pairs={{0,1},{1,2},{2,3},{3,4},{4,5},{5,6},{6,7},{7,8},{8,9},{9,10},{10,1... | collective-permute-start | bytes 393224
  624.3 9.7 %collective-permute-start.1 = (bf16[14,4096]{1,0:T(8,128)(2,1)S(1)}, bf16[14,4096]{1,0:T(8,128)(2,1)S(1)}, u32[]{:S(2)}, u32[]{:S(2)}) collective-permute-start(bf16[14,4096]{1,0:T(8,128)(2,1)S(1)} %slice.20), channel_id=1, source_target_pairs={{0,2},{1,3},{2,4},{3,5},{4,6},{5,7},{6,8},{7,9},{8,10},{9,11},{10,... | collective-permute-start | bytes 344072
Sparse Core Ops, SparseCore 0:
  9.5 73.1 all-gather.1
  156.7 272.4 all-reduce.4

commit v2 on v0

--- a/solution.py
+++ b/solution.py
@@ -73,7 +73,7 @@
     partial_value = lax.dot_general(
         query_vec, passages, (((1,), (1,)), ((), ())), preferred_element_type=jnp.float32
     )
-    scores = score_scale * lax.psum(partial_value, "vocab")
+    scores = score_scale * jnp.sum(lax.all_gather(partial_value, "vocab"), axis=0)
     score_grad = score_grads(scores, positives, pairs_all)
     query_grad = score_scale * jnp.dot(
         score_grad, passages.astype(jnp.float32), precision=lax.Precision.HIGHEST

time: 667 us -> 666 us (level)
    psum x1 -> x0, blocking collectives: 51.4 us -> none  [per_device(): scores = score_scale * lax.psum(partial_value, 'vocab')]
    all_gather x0 -> x1, blocking collectives: none -> 50.2 us  [per_device(): lax.all_gather(partial_value, 'vocab')]
where the time goes in v2:
time: 666 us; the launch traced here: 665 us
  waiting for transfers between devices  350 us (53%)
  blocking collectives  269 us (40%)
  matrix products  14.9 us (2%)
  between operations  14.9 us (2%)
  starting transfers between devices  6.85 us (1%)
    unnamed x5, waiting for transfers between devices  277 us
    unnamed x1, blocking collectives  182 us
    all_gather x1, waiting for transfers between devices, per_device(): weights = lax.all_gather(head_weight, 'dp', axis=0, tiled=True)  72.9 us
    all_gather x1, blocking collectives, per_device(): lax.all_gather(partial_value, 'vocab')  50.2 us
    all_gather x1, blocking collectives, per_device(): passages = lax.all_gather(passage_vec, 'dp', axis=0, tiled=True)  37.5 us
  transfers between devices with their start and end apart: 4, of which 3 were waited for; matrix products, arithmetic and copies ran while one was open for 1% of the time, Pallas kernels for 0%

profile of v2, /device:TPU:94, one launch (start us, length us, event | category | flops | bytes accessed | tf_op | source)
XLA Modules:
  0.0 665.4 jit_solution(11472269314277729454)
XLA Ops:
  6.5 0.7 all-gather.5.cloned.1.call-update
  7.5 1.0 slice_reduce_fusion.3
  8.8 1.0 convert_reduce_fusion.1
  9.9 72.9 %all-gather.5.cloned.1.call-done = bf16[4096,1024]{1,0:T(8,128)(2,1)} async-done(((bf16[128,1024]{1,0:T(8,128)(2,1)}), bf16[4096,1024]{1,0:T(8,128)(2,1)}) %all-gather.5.cloned.1.call-update) | async-done | bytes 8388624 | tf_op jit(solution)/shard_map/all_gather | solution.py:64
  82.7 5.4 convolution_add_fusion
  88.2 0.9 fusion.5
  89.2 37.5 %all-gather.1 = bf16[32,2,1024]{2,1,0:T(2,128)(2,1)S(1)} all-gather(bf16[1,2,1024]{2,1,0:T(2,128)(2,1)S(1)} %fusion.8), channel_id=1, replica_groups=mesh['dp'=32,'vocab'=16] {'dp'}, dimensions={0}, use_global_device_ids=true | all-gather | bytes 135168 | tf_op jit(solution)/shard_map/all_gather | solution.py:72
  126.8 0.2 convolution_bitcast_fusion
  127.0 50.2 %all-gather.2 = f32[16,2,64]{2,1,0:T(2,128)S(1)} all-gather(f32[1,2,64]{2,1,0:T(2,128)S(1)} %convolution_bitcast_fusion), channel_id=2, replica_groups=mesh['dp'=32,'vocab'=16] {'vocab'}, dimensions={0}, use_global_device_ids=true | all-gather | bytes 8704 | tf_op jit(solution)/shard_map/all_gather | solution.py:76
  177.4 0.2 fusion.10
  177.6 1.1 fusion.11
  178.7 1.3 dynamic-slice
  180.6 0.2 fusion.1
  180.9 271.7 %all-reduce.5.cloned.1.call-done = f32[64,1024]{1,0:T(8,128)} async-done(((f32[64,1024]{1,0:T(8,128)}), f32[64,1024]{1,0:T(8,128)}) %all-reduce.5.cloned.1.call-update) | async-done | bytes 262160
  452.6 0.8 fusion.7
  453.5 1.1 fusion.6
  454.7 7.9 %fusion.14 = f32[224,4096]{1,0:T(8,128)} fusion(bf16[224,1024]{1,0:T(8,128)(2,1)S(1)} %fusion.6, bf16[4096,1024]{1,0:T(8,128)(2,1)} %all-gather.5.cloned.1.call-done), kind=kOutput, calls=%fused_computation.38 | convolution fusion | flops 1879048192 | bytes 12517376 | tf_op jit(solution)/shard_map/dot_general | solution.py:97
  462.6 181.7 %fusion = f32[16,4096]{1,0:T(8,128)S(1)} fusion(f32[224,4096]{1,0:T(8,128)} %fusion.14), kind=kCustom, calls=%all-reduce-scatter | all-reduce-scatter fusion | flops 1048577 | bytes 3934208
  644.3 3.3 collective-permute-start
  647.6 3.5 collective-permute-start.1
  651.1 1.3 dynamic-slice.6
  653.1 4.2 collective-permute-done.1
  657.3 0.6 concatenate.7
  657.9 0.7 dynamic-slice_convert_fusion
  (31 shorter events, 1.2 us)
Async XLA Ops:
  6.5 76.2 %copy-start = (bf16[224,4096]{1,0:T(8,128)(2,1)S(1)}, bf16[224,4096]{1,0:T(8,128)(2,1)}, u32[]{:S(2)}) copy-start(bf16[224,4096]{1,0:T(8,128)(2,1)} %param.5) | copy-start | bytes 5505028
  6.5 76.2 %all-gather.5.cloned.1.call-start = ((), (), s32[]{:S(2)}) async-start(), calls=%async_computation | async-start | bytes 8650752 | tf_op jit(solution)/shard_map/all_gather | solution.py:64
  7.3 445.3 %all-reduce.5.cloned.1.call-start = ((), (), s32[]{:S(2)}) async-start(), calls=%async_computation.1 | async-start | bytes 524288
  9.9 167.7 %copy-start.1 = (s32[2]{0:T(128)S(1)}, s32[2]{0:T(128)}, u32[]{:S(2)}) copy-start(s32[2]{0:T(128)} %param.9) | copy-start | bytes 28
  644.3 13.0 %collective-permute-start = (bf16[16,4096]{1,0:T(8,128)(2,1)S(1)}, bf16[16,4096]{1,0:T(8,128)(2,1)S(1)}, u32[]{:S(2)}, u32[]{:S(2)}) collective-permute-start(bf16[16,4096]{1,0:T(8,128)(2,1)S(1)} %convert), channel_id=1, source_target_pairs={{0,1},{1,2},{2,3},{3,4},{4,5},{5,6},{6,7},{7,8},{8,9},{9,10},{10,1... | collective-permute-start | bytes 393224
  647.6 9.7 %collective-permute-start.1 = (bf16[14,4096]{1,0:T(8,128)(2,1)S(1)}, bf16[14,4096]{1,0:T(8,128)(2,1)S(1)}, u32[]{:S(2)}, u32[]{:S(2)}) collective-permute-start(bf16[14,4096]{1,0:T(8,128)(2,1)S(1)} %slice.20), channel_id=1, source_target_pairs={{0,2},{1,3},{2,4},{3,5},{4,6},{5,7},{6,8},{7,9},{8,10},{9,11},{10,... | collective-permute-start | bytes 344072
Sparse Core Ops, SparseCore 0:
  9.5 73.1 all-gather.4
  178.8 273.7 all-reduce.4
